TPU v7x, 128 devices: a whole 4x4x4 slice. The times are simulated.
128 devices in a mesh: sample: 4 (over x_lo, core), space: 4 (over y), chan: 8 (over x_hi, z).
Axes of the slice: x: 4 (x_hi: 2, x_lo: 2; x = x_hi * 2 + x_lo), y: 4, z: 4, core: 2. Of those that a mesh axis runs over, the one named last changes fastest.
Arguments:
- volume: bfloat16 [16, 32, 32, 64, 128], P(None, 'sample', 'space', 'chan'), may hold values from -6 to 6
- fine_kernel: bfloat16 [3, 3, 3, 128, 256], replicated, may hold values from -0.109375 to 0.109375
- fine_bias: float32 [256], replicated, may hold values from -3 to 3
- deep_kernel: bfloat16 [3, 3, 3, 256, 256], replicated, may hold values from -0.078125 to 0.078125
- deep_bias: float32 [256], replicated, may hold values from -3 to 3
Outputs:
- deep_out: bfloat16 [16, 256, 16, 512], P(('sample', 'space'), 'chan')
All inputs are finite; a program needn't handle non-finite values.
Results may differ from a plain program's by a relative error of at most 0.0048.
Values may be sent and summed in bfloat16 or wider, within the bound.
No kernel may reach another device: no remote copies, remote signals or barrier semaphores. Data moves between devices by JAX's collectives and lax.ppermute only.
A program may use at most 256 MiB of HBM per device.

v0:
```python
import jax
import jax.numpy as jnp
import numpy as np
from jax import lax
from jax.experimental import pallas as pl
from jax.experimental.pallas import tpu as pltpu
from jax.sharding import PartitionSpec as P

MIB = 1 << 20
FINE_MIB = 36
BF16 = jnp.bfloat16
F32 = jnp.float32
VMEM = pl.BlockSpec(memory_space=pltpu.VMEM)
ANY = pl.BlockSpec(memory_space=pl.ANY)


def lane_matrix():
    src = np.arange(512).reshape(8, 4, 4, 4)
    dst = src.transpose(1, 2, 0, 3).reshape(-1)
    m = np.zeros((512, 512), np.float32)
    m[dst, np.arange(512)] = 1
    return m


def pad_matrix():
    m = np.zeros((6, 6, 16, 256), np.float32)
    for i in range(6):
        for j in range(6):
            for big in range(4):
                for p in range(4):
                    z, x = (4 * big + i - 1) % 16, (4 * p + j - 1) % 16
                    m[i, j, big * 4 + p, ((z // 4) * 4 + x // 4) * 16 + (z % 4) * 4 + x % 4] = 1
    return m.reshape(576, 256)


def params(mib):
    return pltpu.CompilerParams(vmem_limit_bytes=mib * MIB)


def cost(flops, moved):
    return pl.CostEstimate(flops=flops, bytes_accessed=moved, transcendentals=0)


def leaky(value):
    return jnp.where(value >= 0, value, 0.3 * value)


def dot(a, b):
    return jnp.dot(a, b, preferred_element_type=F32)


def swap_rows():
    i = lax.broadcasted_iota(jnp.int32, (256, 256), 0)
    j = lax.broadcasted_iota(jnp.int32, (256, 256), 1)
    hit = ((i >> 4) == (j & 15)) & ((i & 15) == (j >> 4))
    return jnp.where(hit, 1.0, 0.0).astype(BF16)


def shift(value, axis, step):
    n = lax.axis_size(axis)
    return lax.ppermute(value, axis, [(i, (i + step) % n) for i in range(n)])


def swap_pairs(value, axis, odd):
    n = lax.axis_size(axis)
    pairs = []
    for i in range(n):
        up = (i % 2 == 1) if odd else (i % 2 == 0)
        pairs.append((i, (i + 1) % n if up else (i - 1) % n))
    return lax.ppermute(value, axis, pairs)


def turn(p, slab, put):
    for j in (0, 2):
        halves = [slab[:, (j + k) * 16 : (j + k) * 16 + 16].reshape(256, 128) for k in (0, 1)]
        turned = dot(p, jnp.concatenate(halves, -1)).astype(BF16)
        for k in (0, 1):
            put(2 * (j + k), turned[:, k * 128 : (k + 1) * 128].reshape(2, 128, 128))


def turn_all_kernel(vol, block, lo, hi):
    p = swap_rows()
    for z in (0, 7, 1, 2, 3, 4, 5, 6):

        def put(x, value, z=z):
            block[z, x : x + 2] = value
            if z == 0:
                lo[x : x + 2] = value
            if z == 7:
                hi[x : x + 2] = value

        turn(p, vol[:, z], put)


def turn_all(vol):
    face = jax.ShapeDtypeStruct((8, 128, 128), BF16)
    return pl.pallas_call(
        turn_all_kernel,
        out_shape=[jax.ShapeDtypeStruct((8, 8, 128, 128), BF16), face, face],
        in_specs=[VMEM],
        out_specs=[VMEM] * 3,
        compiler_params=params(12),
        cost_estimate=cost(2 * 8192 * 256 * 256, 4 << 20),
        name="turn_all",
    )(vol)


def pool_inner(acc, z, mid, epool):
    parts = [acc[:, 0:1], jnp.maximum(acc[:, 1:2], acc[:, 2:3]), jnp.maximum(acc[:, 3:4], acc[:, 4:5]), acc[:, 5:6]]
    acc = jnp.concatenate(parts, 1)
    for i in range(acc.shape[0]):
        epool[0, z[i]] = acc[i, :, 0]
        epool[1, z[i]] = acc[i, :, 5]
        for y in (0, 1):
            mid[y, z[i]] = jnp.maximum(acc[i, :, 1 + 2 * y], acc[i, :, 2 + 2 * y])


def tap_rows(planes, dys, first, count):
    return [
        planes(dz, dx, slice((first + dy) * 16, (first + dy + count) * 16))
        for dz in range(3)
        for dx in range(3)
        for dy in dys
    ]


def inner_cells(planes, w):
    taps = [t.reshape(1152, 128) for t in tap_rows(planes, (0, 1, 2), 0, 6)]
    return dot(jnp.concatenate(taps, -1), w[...]).reshape(2, 6, 6, 16, 256)


def edge_rows(w, e):
    first = 128 * (1 - e)
    return jnp.concatenate([w[t * 384 + first : t * 384 + first + 256] for t in range(9)], 0)


def edge_cells(planes, cells, w, eacc):
    for e in (0, 1):
        taps = [t.reshape(cells * 16, 128) for t in tap_rows(planes, (0, 1), 6 * e, 1)]
        acc = dot(jnp.concatenate(taps, -1), edge_rows(w, e))
        eacc[e] = acc.reshape(eacc.shape[1:])


def pooled_f32(pairs):
    return jax.ShapeDtypeStruct((2, pairs, 4, 16, 256), F32)


def fine_call(kernel, outs, name, cells, operands, moved=5 << 20):
    return pl.pallas_call(
        kernel,
        out_shape=outs,
        in_specs=[VMEM] * len(operands),
        out_specs=[VMEM] * len(outs),
        compiler_params=params(FINE_MIB),
        cost_estimate=cost(cells * 16 * 3456 * 256 * 2, moved),
        name=name,
    )(*operands)


def fine_inner_kernel(block, w, mid, epool, eacc):
    def ends(dz, dx, rows):
        return jnp.concatenate([block[z + dz : z + dz + 1, dx : 6 + dx, rows] for z in (0, 5)], 0)

    pool_inner(inner_cells(ends, w), (0, 3), mid, epool)
    for z in (1, 2):

        def pair(dz, dx, rows, z=z):
            return block[2 * z - 1 + dz : 2 * z + 1 + dz, dx : 6 + dx, rows]

        acc = inner_cells(pair, w)
        pool_inner(jnp.maximum(acc[0:1], acc[1:2]), (z,), mid, epool)

    def planes(dz, dx, rows):
        return block[dz : 6 + dz, dx : 6 + dx, rows]

    edge_cells(planes, 36, w, eacc)


def fine_inner(block, w):
    outs = [pooled_f32(4), pooled_f32(4), jax.ShapeDtypeStruct((2, 6, 6, 16, 256), F32)]
    return fine_call(fine_inner_kernel, outs, "fine_inner", 270, (block, w))


def fine_ends_kernel(zlo, block, zhi, w, mid, epool, eacc):
    def planes(dz, dx, rows):
        low = zlo[dx : 6 + dx, rows] if dz == 0 else block[dz - 1, dx : 6 + dx, rows]
        high = zhi[dx : 6 + dx, rows] if dz == 2 else block[6 + dz, dx : 6 + dx, rows]
        return jnp.stack([low, high], 0)

    pool_inner(inner_cells(planes, w), (0, 1), mid, epool)
    edge_cells(planes, 12, w, eacc)


def fine_ends(zlo, block, zhi, w):
    outs = [pooled_f32(2), pooled_f32(2), jax.ShapeDtypeStruct((2, 2, 6, 16, 256), F32)]
    return fine_call(fine_ends_kernel, outs, "fine_ends", 90, (zlo, block, zhi, w))


def emitter(p, out, b):
    def emit(y, plane):
        cells = leaky(plane + b[...]).astype(BF16).reshape(256, 256)
        out[:, pl.ds(y * 16 if isinstance(y, int) else pl.multiple_of(y * 16, 16), 16)] = (
            dot(p, cells).astype(BF16).reshape(16, 16, 256)
        )

    return emit


def fine_sides_kernel(
    xlo, xhi, zlo, block, zhi, w, b, mid_i, epool_i, mid_z, epool_z, outm, epool, eacc
):
    def column(x, dz, rows):
        if dz == 0:
            return jnp.concatenate([zlo[x : x + 1, rows], block[0:7, x, rows]], 0)
        if dz == 1:
            return block[0:8, x, rows]
        return jnp.concatenate([block[1:8, x, rows], zhi[x : x + 1, rows]], 0)

    def planes(dz, dx, rows):
        first = xlo[dz : dz + 8, rows] if dx == 0 else column(dx - 1, dz, rows)
        second = xhi[dz : dz + 8, rows] if dx == 2 else column(6 + dx, dz, rows)
        return jnp.stack([first, second], 1)

    taps = [t.reshape(1536, 128) for t in tap_rows(planes, (0, 1, 2), 0, 6)]
    acc = dot(jnp.concatenate(taps, -1), w[...]).reshape(4, 2, 2, 6, 16, 256).max(axis=1)

    def whole(sides, inner, ends):
        low = jnp.maximum(inner[0:1], ends[0:1])
        high = jnp.maximum(inner[3:4], ends[1:2])
        plane = jnp.concatenate([low, inner[1:3], high], 0)
        first = jnp.maximum(plane[:, 0:1], sides[:, 0:1])
        last = jnp.maximum(plane[:, 3:4], sides[:, 1:2])
        return jnp.concatenate([first, plane[:, 1:3], last], 1)

    for e in (0, 1):
        epool[e] = whole(acc[:, :, 5 * e], epool_i[e], epool_z[e])
    emit = emitter(swap_rows(), outm, b)
    for y in (0, 1):
        inner = jnp.maximum(acc[:, :, 1 + 2 * y], acc[:, :, 2 + 2 * y])
        emit(y, whole(inner, mid_i[y], mid_z[y]))
    edge_cells(planes, 16, w, eacc)


def fine_sides(*operands):
    outs = [
        jax.ShapeDtypeStruct((16, 32, 256), BF16),
        pooled_f32(4),
        jax.ShapeDtypeStruct((2, 8, 2, 16, 256), F32),
    ]
    return fine_call(fine_sides_kernel, outs, "fine_sides", 124, operands)


def fine_faces_kernel(odd, got_a, got_b, w, eacc_i, eacc_z, out, ys):
    ys[...] = jnp.zeros_like(ys)
    for k, (got, e) in enumerate(((got_a, odd[0]), (got_b, 1 - odd[0]))):
        ys[k, 1:9, 1:9] = got[...]
        taps = [ys[k, dz : dz + 8, dx : dx + 8].reshape(1024, 128) for dz in range(3) for dx in range(3)]
        acc = dot(jnp.concatenate(taps, -1), w[:, pl.ds(2 * e, 1)].reshape(1152, 256))
        acc = acc.reshape(8, 8, 16, 256)
        one = pl.ds(e, 1)
        out[one, :, 0] = acc[None, :, 0]
        out[one, :, 7] = acc[None, :, 7]
        out[one, 0, 1:7] = acc[None, 0, 1:7] + eacc_z[one, 0]
        out[one, 1:7, 1:7] = acc[None, 1:7, 1:7] + eacc_i[one]
        out[one, 7, 1:7] = acc[None, 7, 1:7] + eacc_z[one, 1]


def fine_faces(odd, faces, w, eacc_i, eacc_z):
    return pl.pallas_call(
        fine_faces_kernel,
        out_shape=jax.ShapeDtypeStruct((2, 8, 8, 16, 256), F32),
        in_specs=[pl.BlockSpec(memory_space=pltpu.SMEM)] + [VMEM] * 5,
        out_specs=VMEM,
        scratch_shapes=[pltpu.VMEM((2, 10, 10, 16, 128), BF16)],
        compiler_params=params(20),
        cost_estimate=cost(2 * 2048 * 1152 * 256, 6 << 20),
        name="fine_faces",
    )(odd, *faces, w, eacc_i, eacc_z)


def fine_last_kernel(odd, zlo, zhi, xlo, xhi, w, b, facc, outm, epool, eacc, out, sums):
    emit = emitter(swap_rows(), out, b)
    out[:, 16:48] = outm[...]
    zero = jnp.zeros((1, 16, 128), BF16)
    for k, e in enumerate((odd[0], 1 - odd[0])):
        one = pl.ds(e, 1)
        acc = sums.at[k]
        acc[:, 1:7] = facc[one, :, 1:7][0]
        acc[:, 0] = facc[one, :, 0][0] + eacc[one, :, 0][0]
        acc[:, 7] = facc[one, :, 7][0] + eacc[one, :, 1][0]

        def side(cells, taps):
            cells = jnp.concatenate(cells, 0)
            left = jnp.concatenate([cells[t : t + 8].reshape(128, 128) for t in range(3)], -1)
            rows = jnp.concatenate([w[t, pl.ds(2 * e, 1)][0] for t in taps], 0)
            return dot(left, rows).reshape(8, 16, 256)

        c, z = 10 * k, 8 * k
        acc[0] += side([xlo[c : c + 1], zlo[z : z + 8], xhi[c : c + 1]], (0, 1, 2))
        acc[7] += side([xlo[c + 9 : c + 10], zhi[z : z + 8], xhi[c + 9 : c + 10]], (6, 7, 8))
        acc[:, 0] += side([zero, xlo[c + 1 : c + 9], zero], (0, 3, 6))
        acc[:, 7] += side([zero, xhi[c + 1 : c + 9], zero], (2, 5, 8))
        plane = acc[...].reshape(4, 2, 4, 2, 16, 256).max(axis=(1, 3))
        emit(3 * e, jnp.maximum(plane, epool[one][0]))


def fine_last(odd, strips, w, b, facc, sides):
    return pl.pallas_call(
        fine_last_kernel,
        out_shape=jax.ShapeDtypeStruct((16, 64, 256), BF16),
        in_specs=[pl.BlockSpec(memory_space=pltpu.SMEM)] + [VMEM] * 10,
        out_specs=VMEM,
        scratch_shapes=[pltpu.VMEM((2, 8, 8, 16, 256), F32)],
        compiler_params=params(20),
        cost_estimate=cost(2 * 1024 * 384 * 256, 6 << 20),
        name="fine_last",
    )(odd, *strips, w, b, facc, *sides)


def deep_first_kernel(got, pad, w, out, xs):
    for y in range(4):
        plane = got[:, y * 16 : y * 16 + 16].reshape(256, 256)
        xs[y] = dot(pad[...], plane).astype(BF16).reshape(6, 6, 16, 256)

    def part(dy, first, size):
        taps = [
            xs[first : first + size, dz : dz + 4, dx : dx + 4].reshape(256 * size, 256)
            for dz in range(3)
            for dx in range(3)
        ]
        rows = [w[t, dy] for t in range(9)]
        acc = dot(jnp.concatenate(taps, -1), jnp.concatenate(rows, 0))
        return acc.reshape(size, 4, 4, 16, 256)

    out[...] = part(1, 0, 4)
    out[1:4] += part(0, 0, 3)
    out[0:3] += part(2, 1, 3)


def deep_first(got, pad, w):
    return pl.pallas_call(
        deep_first_kernel,
        out_shape=jax.ShapeDtypeStruct((4, 4, 4, 16, 256), F32),
        in_specs=[VMEM] * 3,
        out_specs=VMEM,
        scratch_shapes=[pltpu.VMEM((4, 6, 6, 16, 256), BF16)],
        compiler_params=params(40),
        cost_estimate=cost(2 * 1024 * 6912 * 256, 6 << 20),
        name="deep_first",
    )(got, pad, w)


def deep_last_kernel(odd, got_a, got_b, pad, w, b, acc_in, out, ys, full, turned):
    p = swap_rows()
    for y in (1, 2):
        full[:, :, y] = leaky(acc_in[y] + b[...]).astype(BF16)
    for k, (got, e) in enumerate(((got_a, odd[0]), (got_b, 1 - odd[0]))):
        ys[k] = dot(pad[...], got[...].reshape(256, 256)).astype(BF16).reshape(6, 6, 16, 256)
        taps = [ys[k, dz : dz + 4, dx : dx + 4].reshape(256, 256) for dz in range(3) for dx in range(3)]
        acc = dot(jnp.concatenate(taps, -1), w[:, pl.ds(2 * e, 1)].reshape(2304, 256))
        acc = acc.reshape(4, 4, 16, 256) + acc_in[pl.ds(3 * e, 1)][0]
        full[:, :, pl.ds(3 * e, 1)] = leaky(acc + b[...]).astype(BF16)[:, :, None]
    planes = [dot(p, full[z].reshape(256, 256)).reshape(16, 16, 256) for z in range(4)]
    for k in range(8):
        big, z = k // 4, k % 4
        rows = [planes[z][b4 * 4 : b4 * 4 + 4].reshape(64, 256) for b4 in (big, big + 2)]
        turned[k] = jnp.concatenate(rows, 0).T.astype(BF16).reshape(8, 32, 128)
    i = lax.broadcasted_iota(jnp.int32, (256, 256), 0)
    j = lax.broadcasted_iota(jnp.int32, (256, 256), 1)
    q = jnp.where(((i >> 3) == (j & 31)) & ((i & 7) == (j >> 5)), 1.0, 0.0).astype(BF16)
    for c in (0, 2, 4, 6):
        pair = [turned[:, c + k].reshape(256, 128) for k in (0, 1)]
        moved = dot(q, jnp.concatenate(pair, -1)).astype(BF16)
        for k in (0, 1):
            out[c + k] = moved[:, k * 128 : (k + 1) * 128]


def deep_last(odd, got_a, got_b, pad, w, b, acc):
    return pl.pallas_call(
        deep_last_kernel,
        out_shape=jax.ShapeDtypeStruct((8, 256, 128), BF16),
        in_specs=[pl.BlockSpec(memory_space=pltpu.SMEM)] + [VMEM] * 6,
        out_specs=VMEM,
        scratch_shapes=[
            pltpu.VMEM((2, 6, 6, 16, 256), BF16),
            pltpu.VMEM((4, 4, 4, 16, 256), BF16),
            pltpu.VMEM((8, 8, 32, 128), BF16),
        ],
        compiler_params=params(24),
        cost_estimate=cost(2 * 512 * 2304 * 256, 6 << 20),
        name="deep_last",
    )(odd, got_a, got_b, pad, w, b, acc)


def arrange_kernel(got, lanes, out):
    lane = lax.broadcasted_iota(jnp.int32, (256, 128), 1)
    low, high = [], []
    for c in (0, 2, 4, 6):
        first, second = got[c].astype(F32), got[c + 1].astype(F32)
        low.append(jnp.where(lane < 64, first, pltpu.roll(second, 64, 1)).astype(BF16))
        high.append(jnp.where(lane < 64, pltpu.roll(first, 64, 1), second).astype(BF16))
    halves = [dot(jnp.concatenate(half, -1), lanes[...]).reshape(32, 8, 512) for half in (low, high)]
    out[0] = jnp.concatenate(halves, 1).astype(BF16)


def arrange(got, lanes):
    return pl.pallas_call(
        arrange_kernel,
        out_shape=jax.ShapeDtypeStruct((1, 32, 16, 512), BF16),
        in_specs=[VMEM] * 2,
        out_specs=VMEM,
        compiler_params=params(16),
        cost_estimate=cost(2 * 512 * 512 * 512, 1 << 20),
        name="arrange",
    )(got, lanes)


def on_device(volume, fine_kernel, fine_bias, deep_kernel, deep_bias):
    odd = lax.axis_index("chan") % 2
    is_odd = odd == 1
    flag = odd.astype(jnp.int32).reshape(1)
    vol = volume.reshape(16, 8, 64, 128)

    def y_exchange(head, tail):
        got_a = swap_pairs(jnp.where(is_odd, tail, head), "chan", True)
        got_b = swap_pairs(jnp.where(is_odd, head, tail), "chan", False)
        return got_a, got_b

    block, tlo, thi = turn_all(vol)
    zlo, zhi = shift(thi, "sample", 1), shift(tlo, "sample", -1)
    got_a, got_b = y_exchange(block[:, :, 0:16], block[:, :, 112:128])
    w = fine_kernel.reshape(3456, 256)
    w9 = fine_kernel.reshape(9, 3, 128, 256)
    b = fine_bias.reshape(1, 256)
    mid_i, epool_i, eacc_i = fine_inner(block, w)

    def x_face(x):
        return jnp.concatenate([zlo[x : x + 1], block[:, x], zhi[x : x + 1]], 0)

    xlo, xhi = shift(x_face(7), "space", 1), shift(x_face(0), "space", -1)
    mid_z, epool_z, eacc_z = fine_ends(zlo, block, zhi, w)
    rzlo = shift(jnp.concatenate([got_a[7], got_b[7]], 0), "sample", 1)
    rzhi = shift(jnp.concatenate([got_a[0], got_b[0]], 0), "sample", -1)
    facc = fine_faces(flag, (got_a, got_b), w9, eacc_i, eacc_z)
    def rim(x):
        return jnp.concatenate(
            [rzlo[x : x + 1], got_a[:, x], rzhi[x : x + 1], rzlo[8 + x : 9 + x], got_b[:, x], rzhi[8 + x : 9 + x]], 0
        )

    rxlo, rxhi = shift(rim(7), "space", 1), shift(rim(0), "space", -1)
    sides = fine_sides(xlo, xhi, zlo, block, zhi, w, b, mid_i, epool_i, mid_z, epool_z)
    send = fine_last(flag, (rzlo, rzhi, rxlo, rxhi), w9, b, facc, sides)
    got = lax.all_to_all(send, ("sample", "space"), split_axis=0, concat_axis=0, tiled=True)

    got_a, got_b = y_exchange(got[:, 0:16], got[:, 48:64])
    pad = jnp.asarray(pad_matrix(), BF16)
    dw = deep_kernel.reshape(9, 3, 256, 256)
    acc = deep_first(got, pad, dw)
    send = deep_last(flag, got_a, got_b, pad, dw, deep_bias.reshape(1, 256), acc)
    got = lax.all_to_all(send, "chan", split_axis=0, concat_axis=0, tiled=True)
    return arrange(got, jnp.asarray(lane_matrix(), BF16))


def solution(mesh):
    placed = (P(None, "sample", "space", "chan", None), P(), P(), P(), P())
    return jax.shard_map(
        on_device,
        mesh=mesh,
        in_specs=placed,
        out_specs=P(("sample", "space"), "chan", None, None),
        check_vma=False,
    )
```

profile of v0, /device:TPU:0, one launch (start us, length us, event | category | flops | bytes accessed | tf_op | source)
XLA Modules:
  0.0 80.9 jit_solution(7408240730431694410)
XLA Ops:
  0.0 0.0 copy-start.6
  0.0 1.6 %copy-done.6 = bf16[16,8,8,8,128]{4,3,2,1,0:T(8,128)(2,1)S(1)} copy-done((bf16[16,8,8,8,128]{4,3,2,1,0:T(8,128)(2,1)S(1)}, bf16[16,8,8,8,128]{4,3,2,1,0:T(8,128)(2,1)}, u32[]{:S(2)}) %copy-start.6) | copy-done | bytes 2097176
  1.6 0.0 copy-start
  1.6 0.7 turn_all.1
  2.4 6.7 %collective-permute-start = (bf16[8,8,16,128]{3,2,1,0:T(8,128)(2,1)S(1)}, bf16[8,8,16,128]{3,2,1,0:T(8,128)(2,1)S(1)}, u32[]{:S(2)}, u32[]{:S(2)}) collective-permute-start(bf16[8,8,16,128]{3,2,1,0:T(8,128)(2,1)S(1)} %get-tuple-element.31), channel_id=1, source_target_pairs={{0,7},{1,2},{2,1},{3,4},{4,3},{5,6},{6,5},{7,0},{8,15},{9,10},{10,... | collective-permute-start | bytes 786440 | tf_op jit(solution)/shard_map/ppermute | solution.py:70
  9.0 0.0 collective-permute-start.1
  9.0 0.0 collective-permute-start.6
  9.0 1.7 %collective-permute-start.7 = (bf16[8,128,128]{2,1,0:T(8,128)(2,1)S(1)}, bf16[8,128,128]{2,1,0:T(8,128)(2,1)S(1)}, u32[]{:S(2)}, u32[]{:S(2)}) collective-permute-start(bf16[8,128,128]{2,1,0:T(8,128)(2,1)S(1)} %get-tuple-element.20), channel_id=1, source_target_pairs={{0,96},{32,0},{64,32},{96,64},{1,97},{33,1},{65,33},{97,65},{2,98}... | collective-permute-start | bytes 786440 | tf_op jit(solution)/shard_map/ppermute | solution.py:61
  10.8 0.0 copy-done
  10.8 8.0 %fine_inner.1 = (f32[2,4,4,16,256]{4,3,2,1,0:T(8,128)S(1)}, f32[2,4,4,16,256]{4,3,2,1,0:T(8,128)S(1)}, f32[2,6,6,16,256]{4,3,2,1,0:T(8,128)S(1)}) custom-call(bf16[8,8,128,128]{3,2,1,0:T(8,128)(2,1)S(1)} %get-tuple-element.17.block, bf16[3456,256]{1,0:T(8,128)(2,1)S(1)} %bitcast.35), custom_call_target="tpu_custom_call" | custom-call | flops 7644119040 | bytes 5242880 | tf_op jit(solution)/shard_map/fine_inner/pallas_call | solution.py:149
  18.9 0.0 collective-permute-done.got_a
  18.9 0.0 collective-permute-done.1.got_b
  18.9 0.1 collective-permute-start.2
  19.0 1.8 %collective-permute-start.3 = (bf16[16,16,128]{2,1,0:T(8,128)(2,1)S(1)}, bf16[16,16,128]{2,1,0:T(8,128)(2,1)S(1)}, u32[]{:S(2)}, u32[]{:S(2)}) collective-permute-start(bf16[16,16,128]{2,1,0:T(8,128)(2,1)S(1)} %pad_maximum_fusion.3), channel_id=1, source_target_pairs={{0,96},{32,0},{64,32},{96,64},{1,97},{33,1},{65,33},{97,65},{2,98}... | collective-permute-start | bytes 196616 | tf_op jit(solution)/shard_map/ppermute | solution.py:61
  20.8 0.0 collective-permute-done.6.zlo
  20.8 0.0 collective-permute-done.7.zhi
  20.9 1.6 %collective-permute-start.8 = (bf16[10,128,128]{2,1,0:T(8,128)(2,1)S(1)}, bf16[10,128,128]{2,1,0:T(8,128)(2,1)S(1)}, u32[]{:S(2)}, u32[]{:S(2)}) collective-permute-start(bf16[10,128,128]{2,1,0:T(8,128)(2,1)S(1)} %pad_maximum_fusion), channel_id=1, source_target_pairs={{0,8},{8,16},{16,24},{24,0},{1,9},{9,17},{17,25},{25,1},{2,10},{10... | collective-permute-start | bytes 983048 | tf_op jit(solution)/shard_map/ppermute | solution.py:61
  22.6 1.9 %collective-permute-start.9 = (bf16[10,128,128]{2,1,0:T(8,128)(2,1)S(1)}, bf16[10,128,128]{2,1,0:T(8,128)(2,1)S(1)}, u32[]{:S(2)}, u32[]{:S(2)}) collective-permute-start(bf16[10,128,128]{2,1,0:T(8,128)(2,1)S(1)} %pad_maximum_fusion.1), channel_id=1, source_target_pairs={{0,24},{8,0},{16,8},{24,16},{1,25},{9,1},{17,9},{25,17},{2,26},{10... | collective-permute-start | bytes 983048 | tf_op jit(solution)/shard_map/ppermute | solution.py:61
  24.5 2.8 %fine_ends.1 = (f32[2,2,4,16,256]{4,3,2,1,0:T(8,128)S(1)}, f32[2,2,4,16,256]{4,3,2,1,0:T(8,128)S(1)}, f32[2,2,6,16,256]{4,3,2,1,0:T(8,128)S(1)}) custom-call(bf16[8,128,128]{2,1,0:T(8,128)(2,1)S(1)} %collective-permute-done.6.zlo, bf16[8,8,128,128]{3,2,1,0:T(8,128)(2,1)S(1)} %get-tuple-element.17.block, bf16[8,128,128]{2,1,0:T(8,128)(2,1)S(1)} %collective-permute-done.7.zhi, ...), custom_call_target="tpu_custom_call" | custom-call | flops 2548039680 | bytes 5242880 | tf_op jit(solution)/shard_map/fine_ends/pallas_call | solution.py:149
  27.3 0.0 copy-start.5
  27.3 1.7 %fine_faces.1.facc = f32[2,8,8,16,256]{4,3,2,1,0:T(8,128)S(1)} custom-call(s32[1]{0:T(128)} %bitcast.odd, bf16[8,8,16,128]{3,2,1,0:T(8,128)(2,1)S(1)} %collective-permute-done.got_a, bf16[8,8,16,128]{3,2,1,0:T(8,128)(2,1)S(1)} %collective-permute-done.1.got_b, bf16[9,3,128,256]{3,2,1,0:T(8,128)(2,1)S(1)} %bitcast.37, ...), custom_call_target="tpu_custom_call" | custom-call | flops 1207959552 | bytes 6291456 | tf_op jit(solution)/shard_map/fine_faces/pallas_call | solution.py:269
  29.0 0.0 collective-permute-done.2.zlo
  29.1 0.0 collective-permute-done.3.zhi
  29.1 0.4 collective-permute-start.4
  29.6 2.9 %collective-permute-start.5 = (bf16[20,16,128]{2,1,0:T(8,128)(2,1)S(1)}, bf16[20,16,128]{2,1,0:T(8,128)(2,1)S(1)}, u32[]{:S(2)}, u32[]{:S(2)}) collective-permute-start(bf16[20,16,128]{2,1,0:T(8,128)(2,1)S(1)} %get-tuple-element.47), channel_id=1, source_target_pairs={{0,24},{8,0},{16,8},{24,16},{1,25},{9,1},{17,9},{25,17},{2,26},{10... | collective-permute-start | bytes 245768 | tf_op jit(solution)/shard_map/ppermute | solution.py:61
  32.4 0.0 collective-permute-done.8.xlo
  32.5 0.7 collective-permute-done.9.xhi
  33.1 0.0 copy-done.5
  33.1 5.2 %fine_sides.1 = (bf16[16,32,256]{2,1,0:T(8,128)(2,1)S(1)}, f32[2,4,4,16,256]{4,3,2,1,0:T(8,128)S(1)}, f32[2,8,2,16,256]{4,3,2,1,0:T(8,128)S(1)}) custom-call(bf16[10,128,128]{2,1,0:T(8,128)(2,1)S(1)} %collective-permute-done.8.xlo, bf16[10,128,128]{2,1,0:T(8,128)(2,1)S(1)} %collective-permute-done.9.xhi, ...), custom_call_target="tpu_custom_call" | custom-call | flops 3510632448 | bytes 5242880 | tf_op jit(solution)/shard_map/fine_sides/pallas_call | solution.py:149
  38.4 0.0 collective-permute-done.4.xlo
  38.4 0.0 collective-permute-done.5.xhi
  38.4 0.0 copy-start.1
  38.4 0.0 copy-start.3
  38.4 0.7 fine_last.1
  39.2 15.3 %all_to_all.10.got = bf16[16,64,256]{2,1,0:T(8,128)(2,1)S(1)} all-to-all(bf16[16,64,256]{2,1,0:T(8,128)(2,1)S(1)} %fine_last.1), channel_id=1, replica_groups=mesh['sample'=4,'space'=4,'chan'=8] {'sample','space'}, dimensions={0} | all-to-all | bytes 1048576 | tf_op jit(solution)/shard_map/all_to_all | solution.py:453
  54.5 2.3 %collective-permute-start.10 = (bf16[16,16,256]{2,1,0:T(8,128)(2,1)S(1)}, bf16[16,16,256]{2,1,0:T(8,128)(2,1)S(1)}, u32[]{:S(2)}, u32[]{:S(2)}) collective-permute-start(bf16[16,16,256]{2,1,0:T(8,128)(2,1)S(1)} %get-tuple-element.34), channel_id=1, source_target_pairs={{0,7},{1,2},{2,1},{3,4},{4,3},{5,6},{6,5},{7,0},{8,15},{9,10},{10,... | collective-permute-start | bytes 393224 | tf_op jit(solution)/shard_map/ppermute | solution.py:70
  56.8 0.0 collective-permute-start.11
  56.8 0.0 copy-done.1
  56.8 0.0 copy-done.3
  56.8 0.0 copy-start.4
  56.8 3.5 %deep_first.1.acc_in = f32[4,4,4,16,256]{4,3,2,1,0:T(8,128)S(1)} custom-call(bf16[16,64,256]{2,1,0:T(8,128)(2,1)S(1)} %all_to_all.10.got, bf16[576,256]{1,0:T(8,128)(2,1)S(1)} %copy-done.3, bf16[9,3,256,256]{3,2,1,0:T(8,128)(2,1)S(1)} %bitcast.40), custom_call_target="tpu_custom_call" | custom-call | flops 3623878656 | bytes 6291456 | tf_op jit(solution)/shard_map/deep_first/pallas_call | solution.py:341
  60.4 3.2 %collective-permute-done.10.got_a = bf16[16,16,256]{2,1,0:T(8,128)(2,1)S(1)} collective-permute-done((bf16[16,16,256]{2,1,0:T(8,128)(2,1)S(1)}, bf16[16,16,256]{2,1,0:T(8,128)(2,1)S(1)}, u32[]{:S(2)}, u32[]{:S(2)}) %collective-permute-start.10) | collective-permute-done | bytes 131104 | tf_op jit(solution)/shard_map/ppermute | solution.py:70
  63.6 0.0 collective-permute-done.11.got_b
  63.6 0.0 copy-done.4
  63.6 1.9 %deep_last.1 = bf16[8,256,128]{2,1,0:T(8,128)(2,1)S(1)} custom-call(s32[1]{0:T(128)} %bitcast.odd, bf16[16,16,256]{2,1,0:T(8,128)(2,1)S(1)} %collective-permute-done.10.got_a, bf16[16,16,256]{2,1,0:T(8,128)(2,1)S(1)} %collective-permute-done.11.got_b, bf16[576,256]{1,0:T(8,128)(2,1)S(1)} %copy-done.3, bf16[9,3,256,256]{3,2,1,0:T(8,128)(2,1)S(1)} %bitcast.41, ...), custom_call_target="tpu_custom_call" | custom-call | flops 603979776 | bytes 6291456 | tf_op jit(solution)/shard_map/deep_last/pallas_call | solution.py:379
  65.5 14.1 %all_to_all.11.got = bf16[8,256,128]{2,1,0:T(8,128)(2,1)S(1)} all-to-all(bf16[8,256,128]{2,1,0:T(8,128)(2,1)S(1)} %deep_last.1), channel_id=1, replica_groups=mesh['sample'=4,'space'=4,'chan'=8] {'chan'}, dimensions={0} | all-to-all | bytes 1048576 | tf_op jit(solution)/shard_map/all_to_all | solution.py:460
  79.6 0.0 copy-done.2
  79.6 1.3 %arrange.1 = bf16[1,32,16,512]{3,2,1,0:T(8,128)(2,1)} custom-call(bf16[8,256,128]{2,1,0:T(8,128)(2,1)S(1)} %all_to_all.11.got, bf16[512,512]{1,0:T(8,128)(2,1)S(1)} %copy-done.2), custom_call_target="tpu_custom_call" | custom-call | flops 268435456 | bytes 1048576 | tf_op jit(solution)/shard_map/arrange/pallas_call | solution.py:407
  (18 shorter events, 0.3 us)
Async XLA Ops:
  0.0 1.6 %copy-start.6 = (bf16[16,8,8,8,128]{4,3,2,1,0:T(8,128)(2,1)S(1)}, bf16[16,8,8,8,128]{4,3,2,1,0:T(8,128)(2,1)}, u32[]{:S(2)}) copy-start(bf16[16,8,8,8,128]{4,3,2,1,0:T(8,128)(2,1)} %param.7) | copy-start | bytes 6291460
  1.6 9.2 %copy-start = (bf16[3,3,3,128,256]{4,3,2,1,0:T(8,128)(2,1)S(1)}, bf16[3,3,3,128,256]{4,3,2,1,0:T(8,128)(2,1)}, u32[]{:S(2)}) copy-start(bf16[3,3,3,128,256]{4,3,2,1,0:T(8,128)(2,1)} %param.8) | copy-start | bytes 5308420
  2.4 16.5 %collective-permute-start = (bf16[8,8,16,128]{3,2,1,0:T(8,128)(2,1)S(1)}, bf16[8,8,16,128]{3,2,1,0:T(8,128)(2,1)S(1)}, u32[]{:S(2)}, u32[]{:S(2)}) collective-permute-start(bf16[8,8,16,128]{3,2,1,0:T(8,128)(2,1)S(1)} %get-tuple-element.31), channel_id=1, source_target_pairs={{0,7},{1,2},{2,1},{3,4},{4,3},{5,6},{6,5},{7,0},{8,15},{9,10},{10,... | collective-permute-start | bytes 786440 | tf_op jit(solution)/shard_map/ppermute | solution.py:70
  9.0 9.9 %collective-permute-start.1 = (bf16[8,8,16,128]{3,2,1,0:T(8,128)(2,1)S(1)}, bf16[8,8,16,128]{3,2,1,0:T(8,128)(2,1)S(1)}, u32[]{:S(2)}, u32[]{:S(2)}) collective-permute-start(bf16[8,8,16,128]{3,2,1,0:T(8,128)(2,1)S(1)} %get-tuple-element.32), channel_id=1, source_target_pairs={{0,1},{1,0},{2,3},{3,2},{4,5},{5,4},{6,7},{7,6},{8,9},{9,8},{10,11... | collective-permute-start | bytes 786440 | tf_op jit(solution)/shard_map/ppermute | solution.py:70
  9.0 11.8 %collective-permute-start.6 = (bf16[8,128,128]{2,1,0:T(8,128)(2,1)S(1)}, bf16[8,128,128]{2,1,0:T(8,128)(2,1)S(1)}, u32[]{:S(2)}, u32[]{:S(2)}) collective-permute-start(bf16[8,128,128]{2,1,0:T(8,128)(2,1)S(1)} %get-tuple-element.19), channel_id=1, source_target_pairs={{0,32},{32,64},{64,96},{96,0},{1,33},{33,65},{65,97},{97,1},{2,34}... | collective-permute-start | bytes 786440 | tf_op jit(solution)/shard_map/ppermute | solution.py:61
  9.0 11.8 %collective-permute-start.7 = (bf16[8,128,128]{2,1,0:T(8,128)(2,1)S(1)}, bf16[8,128,128]{2,1,0:T(8,128)(2,1)S(1)}, u32[]{:S(2)}, u32[]{:S(2)}) collective-permute-start(bf16[8,128,128]{2,1,0:T(8,128)(2,1)S(1)} %get-tuple-element.20), channel_id=1, source_target_pairs={{0,96},{32,0},{64,32},{96,64},{1,97},{33,1},{65,33},{97,65},{2,98}... | collective-permute-start | bytes 786440 | tf_op jit(solution)/shard_map/ppermute | solution.py:61
  18.9 10.1 %collective-permute-start.2 = (bf16[16,16,128]{2,1,0:T(8,128)(2,1)S(1)}, bf16[16,16,128]{2,1,0:T(8,128)(2,1)S(1)}, u32[]{:S(2)}, u32[]{:S(2)}) collective-permute-start(bf16[16,16,128]{2,1,0:T(8,128)(2,1)S(1)} %pad_maximum_fusion.2), channel_id=1, source_target_pairs={{0,32},{32,64},{64,96},{96,0},{1,33},{33,65},{65,97},{97,1},{2,34}... | collective-permute-start | bytes 196616 | tf_op jit(solution)/shard_map/ppermute | solution.py:61
  19.0 10.0 %collective-permute-start.3 = (bf16[16,16,128]{2,1,0:T(8,128)(2,1)S(1)}, bf16[16,16,128]{2,1,0:T(8,128)(2,1)S(1)}, u32[]{:S(2)}, u32[]{:S(2)}) collective-permute-start(bf16[16,16,128]{2,1,0:T(8,128)(2,1)S(1)} %pad_maximum_fusion.3), channel_id=1, source_target_pairs={{0,96},{32,0},{64,32},{96,64},{1,97},{33,1},{65,33},{97,65},{2,98}... | collective-permute-start | bytes 196616 | tf_op jit(solution)/shard_map/ppermute | solution.py:61
  20.9 11.5 %collective-permute-start.8 = (bf16[10,128,128]{2,1,0:T(8,128)(2,1)S(1)}, bf16[10,128,128]{2,1,0:T(8,128)(2,1)S(1)}, u32[]{:S(2)}, u32[]{:S(2)}) collective-permute-start(bf16[10,128,128]{2,1,0:T(8,128)(2,1)S(1)} %pad_maximum_fusion), channel_id=1, source_target_pairs={{0,8},{8,16},{16,24},{24,0},{1,9},{9,17},{17,25},{25,1},{2,10},{10... | collective-permute-start | bytes 983048 | tf_op jit(solution)/shard_map/ppermute | solution.py:61
  22.6 10.5 %collective-permute-start.9 = (bf16[10,128,128]{2,1,0:T(8,128)(2,1)S(1)}, bf16[10,128,128]{2,1,0:T(8,128)(2,1)S(1)}, u32[]{:S(2)}, u32[]{:S(2)}) collective-permute-start(bf16[10,128,128]{2,1,0:T(8,128)(2,1)S(1)} %pad_maximum_fusion.1), channel_id=1, source_target_pairs={{0,24},{8,0},{16,8},{24,16},{1,25},{9,1},{17,9},{25,17},{2,26},{10... | collective-permute-start | bytes 983048 | tf_op jit(solution)/shard_map/ppermute | solution.py:61
  27.3 5.8 %copy-start.5 = (f32[256]{0:T(256)S(1)}, f32[256]{0:T(256)}, u32[]{:S(2)}) copy-start(f32[256]{0:T(256)} %param.9) | copy-start | bytes 3076
  29.1 9.2 %collective-permute-start.4 = (bf16[20,16,128]{2,1,0:T(8,128)(2,1)S(1)}, bf16[20,16,128]{2,1,0:T(8,128)(2,1)S(1)}, u32[]{:S(2)}, u32[]{:S(2)}) collective-permute-start(bf16[20,16,128]{2,1,0:T(8,128)(2,1)S(1)} %get-tuple-element.48), channel_id=1, source_target_pairs={{0,8},{8,16},{16,24},{24,0},{1,9},{9,17},{17,25},{25,1},{2,10},{10... | collective-permute-start | bytes 245768 | tf_op jit(solution)/shard_map/ppermute | solution.py:61
  29.6 8.8 %collective-permute-start.5 = (bf16[20,16,128]{2,1,0:T(8,128)(2,1)S(1)}, bf16[20,16,128]{2,1,0:T(8,128)(2,1)S(1)}, u32[]{:S(2)}, u32[]{:S(2)}) collective-permute-start(bf16[20,16,128]{2,1,0:T(8,128)(2,1)S(1)} %get-tuple-element.47), channel_id=1, source_target_pairs={{0,24},{8,0},{16,8},{24,16},{1,25},{9,1},{17,9},{25,17},{2,26},{10... | collective-permute-start | bytes 245768 | tf_op jit(solution)/shard_map/ppermute | solution.py:61
  38.4 18.4 %copy-start.1 = (bf16[3,3,3,256,256]{4,3,2,1,0:T(8,128)(2,1)S(1)}, bf16[3,3,3,256,256]{4,3,2,1,0:T(8,128)(2,1)}, u32[]{:S(2)}) copy-start(bf16[3,3,3,256,256]{4,3,2,1,0:T(8,128)(2,1)} %param.10) | copy-start | bytes 10616836
  38.4 18.4 %copy-start.3 = (bf16[576,256]{1,0:T(8,128)(2,1)S(1)}, bf16[576,256]{1,0:T(8,128)(2,1)}, u32[]{:S(2)}) copy-start(bf16[576,256]{1,0:T(8,128)(2,1)} %constant.22.clone.pad) | copy-start | bytes 884740
  54.5 9.0 %collective-permute-start.10 = (bf16[16,16,256]{2,1,0:T(8,128)(2,1)S(1)}, bf16[16,16,256]{2,1,0:T(8,128)(2,1)S(1)}, u32[]{:S(2)}, u32[]{:S(2)}) collective-permute-start(bf16[16,16,256]{2,1,0:T(8,128)(2,1)S(1)} %get-tuple-element.34), channel_id=1, source_target_pairs={{0,7},{1,2},{2,1},{3,4},{4,3},{5,6},{6,5},{7,0},{8,15},{9,10},{10,... | collective-permute-start | bytes 393224 | tf_op jit(solution)/shard_map/ppermute | solution.py:70
  56.8 6.7 %collective-permute-start.11 = (bf16[16,16,256]{2,1,0:T(8,128)(2,1)S(1)}, bf16[16,16,256]{2,1,0:T(8,128)(2,1)S(1)}, u32[]{:S(2)}, u32[]{:S(2)}) collective-permute-start(bf16[16,16,256]{2,1,0:T(8,128)(2,1)S(1)} %get-tuple-element.33), channel_id=1, source_target_pairs={{0,1},{1,0},{2,3},{3,2},{4,5},{5,4},{6,7},{7,6},{8,9},{9,8},{10,11... | collective-permute-start | bytes 393224 | tf_op jit(solution)/shard_map/ppermute | solution.py:70
  56.8 6.7 %copy-start.4 = (f32[256]{0:T(256)S(1)}, f32[256]{0:T(256)}, u32[]{:S(2)}) copy-start(f32[256]{0:T(256)} %param.11) | copy-start | bytes 3076
  63.6 16.0 %copy-start.2 = (bf16[512,512]{1,0:T(8,128)(2,1)S(1)}, bf16[512,512]{1,0:T(8,128)(2,1)}, u32[]{:S(2)}) copy-start(bf16[512,512]{1,0:T(8,128)(2,1)} %constant.23.clone.lanes) | copy-start | bytes 1572868
where the time goes:
time: 81 us; the launch traced here: 80.9 us
  blocking collectives  29.4 us (36%)
  Pallas kernels  25.9 us (32%)
  starting transfers between devices  19.5 us (24%)
  waiting for transfers between devices  3.89 us (5%)
  local copies, waits for them, and re-layouts  1.75 us (2%)
    pallas_call x3, Pallas kernels, fine_call(): pl.pallas_call(kernel, out_shape=outs, in_specs=[VMEM] * len(operands), o...  16.1 us
    all_to_all x1, blocking collectives, on_device(): lax.all_to_all(send, ('sample', 'space'), split_axis=0, concat_axis=0, ti...  15.3 us
    all_to_all x1, blocking collectives, on_device(): got = lax.all_to_all(send, 'chan', split_axis=0, concat_axis=0, tiled=True)  14.1 us
    ppermute x8, starting transfers between devices, shift(): return lax.ppermute(value, axis, [(i, (i + step) % n) for i in range(n)])  10.5 us
    ppermute x4, starting transfers between devices, swap_pairs(): return lax.ppermute(value, axis, pairs)  8.98 us
    pallas_call x1, Pallas kernels, deep_first(): pl.pallas_call(deep_first_kernel, out_shape=jax.ShapeDtypeStruct((4, 4, 4...  3.52 us
    ppermute x4, waiting for transfers between devices, swap_pairs(): return lax.ppermute(value, axis, pairs)  3.19 us
    pallas_call x1, Pallas kernels, deep_last(): pl.pallas_call(deep_last_kernel, out_shape=jax.ShapeDtypeStruct((8, 256,...  1.91 us
  transfers between devices with their start and end apart: 12, of which 2 were waited for; matrix products, arithmetic and copies ran while one was open for 0% of the time, Pallas kernels for 26%

commit v1 on v0

--- a/solution.py
+++ b/solution.py
@@ -364,7 +364,7 @@
     for k in range(8):
         big, z = k // 4, k % 4
         rows = [planes[z][b4 * 4 : b4 * 4 + 4].reshape(64, 256) for b4 in (big, big + 2)]
-        turned[k] = jnp.concatenate(rows, 0).T.astype(BF16).reshape(8, 32, 128)
+        turned[k] = jnp.concatenate(rows, 0).astype(BF16).T.reshape(8, 32, 128)
     i = lax.broadcasted_iota(jnp.int32, (256, 256), 0)
     j = lax.broadcasted_iota(jnp.int32, (256, 256), 1)
     q = jnp.where(((i >> 3) == (j & 31)) & ((i & 7) == (j >> 5)), 1.0, 0.0).astype(BF16)

time: 81 us -> 81 us (level)
  no operation moved by 1% of the time
where the time goes in v1:
time: 81 us; the launch traced here: 80.9 us
  blocking collectives  29.4 us (36%)
  Pallas kernels  25.9 us (32%)
  starting transfers between devices  19.5 us (24%)
  waiting for transfers between devices  3.89 us (5%)
  local copies, waits for them, and re-layouts  1.75 us (2%)
    pallas_call x3, Pallas kernels, fine_call(): pl.pallas_call(kernel, out_shape=outs, in_specs=[VMEM] * len(operands), o...  16.1 us
    all_to_all x1, blocking collectives, on_device(): lax.all_to_all(send, ('sample', 'space'), split_axis=0, concat_axis=0, ti...  15.3 us
    all_to_all x1, blocking collectives, on_device(): got = lax.all_to_all(send, 'chan', split_axis=0, concat_axis=0, tiled=True)  14.1 us
    ppermute x8, starting transfers between devices, shift(): return lax.ppermute(value, axis, [(i, (i + step) % n) for i in range(n)])  10.5 us
    ppermute x4, starting transfers between devices, swap_pairs(): return lax.ppermute(value, axis, pairs)  8.98 us
    pallas_call x1, Pallas kernels, deep_first(): pl.pallas_call(deep_first_kernel, out_shape=jax.ShapeDtypeStruct((4, 4, 4...  3.52 us
    ppermute x4, waiting for transfers between devices, swap_pairs(): return lax.ppermute(value, axis, pairs)  3.19 us
    pallas_call x1, Pallas kernels, deep_last(): pl.pallas_call(deep_last_kernel, out_shape=jax.ShapeDtypeStruct((8, 256,...  1.9 us
  transfers between devices with their start and end apart: 12, of which 2 were waited for; matrix products, arithmetic and copies ran while one was open for 0% of the time, Pallas kernels for 26%

profile of v1, /device:TPU:0, one launch (start us, length us, event | category | flops | bytes accessed | tf_op | source)
XLA Modules:
  0.0 80.9 jit_solution(322225891107593775)
XLA Ops:
  0.0 0.0 copy-start.6
  0.0 1.6 %copy-done.6 = bf16[16,8,8,8,128]{4,3,2,1,0:T(8,128)(2,1)S(1)} copy-done((bf16[16,8,8,8,128]{4,3,2,1,0:T(8,128)(2,1)S(1)}, bf16[16,8,8,8,128]{4,3,2,1,0:T(8,128)(2,1)}, u32[]{:S(2)}) %copy-start.6) | copy-done | bytes 2097176
  1.6 0.0 copy-start
  1.6 0.7 turn_all.1
  2.4 6.7 %collective-permute-start = (bf16[8,8,16,128]{3,2,1,0:T(8,128)(2,1)S(1)}, bf16[8,8,16,128]{3,2,1,0:T(8,128)(2,1)S(1)}, u32[]{:S(2)}, u32[]{:S(2)}) collective-permute-start(bf16[8,8,16,128]{3,2,1,0:T(8,128)(2,1)S(1)} %get-tuple-element.31), channel_id=1, source_target_pairs={{0,7},{1,2},{2,1},{3,4},{4,3},{5,6},{6,5},{7,0},{8,15},{9,10},{10,... | collective-permute-start | bytes 786440 | tf_op jit(solution)/shard_map/ppermute | solution.py:70
  9.0 0.0 collective-permute-start.1
  9.0 0.0 collective-permute-start.6
  9.0 1.7 %collective-permute-start.7 = (bf16[8,128,128]{2,1,0:T(8,128)(2,1)S(1)}, bf16[8,128,128]{2,1,0:T(8,128)(2,1)S(1)}, u32[]{:S(2)}, u32[]{:S(2)}) collective-permute-start(bf16[8,128,128]{2,1,0:T(8,128)(2,1)S(1)} %get-tuple-element.20), channel_id=1, source_target_pairs={{0,96},{32,0},{64,32},{96,64},{1,97},{33,1},{65,33},{97,65},{2,98}... | collective-permute-start | bytes 786440 | tf_op jit(solution)/shard_map/ppermute | solution.py:61
  10.8 0.0 copy-done
  10.8 8.0 %fine_inner.1 = (f32[2,4,4,16,256]{4,3,2,1,0:T(8,128)S(1)}, f32[2,4,4,16,256]{4,3,2,1,0:T(8,128)S(1)}, f32[2,6,6,16,256]{4,3,2,1,0:T(8,128)S(1)}) custom-call(bf16[8,8,128,128]{3,2,1,0:T(8,128)(2,1)S(1)} %get-tuple-element.17.block, bf16[3456,256]{1,0:T(8,128)(2,1)S(1)} %bitcast.35), custom_call_target="tpu_custom_call" | custom-call | flops 7644119040 | bytes 5242880 | tf_op jit(solution)/shard_map/fine_inner/pallas_call | solution.py:149
  18.9 0.0 collective-permute-done.got_a
  18.9 0.0 collective-permute-done.1.got_b
  18.9 0.1 collective-permute-start.2
  19.0 1.8 %collective-permute-start.3 = (bf16[16,16,128]{2,1,0:T(8,128)(2,1)S(1)}, bf16[16,16,128]{2,1,0:T(8,128)(2,1)S(1)}, u32[]{:S(2)}, u32[]{:S(2)}) collective-permute-start(bf16[16,16,128]{2,1,0:T(8,128)(2,1)S(1)} %pad_maximum_fusion.3), channel_id=1, source_target_pairs={{0,96},{32,0},{64,32},{96,64},{1,97},{33,1},{65,33},{97,65},{2,98}... | collective-permute-start | bytes 196616 | tf_op jit(solution)/shard_map/ppermute | solution.py:61
  20.8 0.0 collective-permute-done.6.zlo
  20.8 0.0 collective-permute-done.7.zhi
  20.9 1.6 %collective-permute-start.8 = (bf16[10,128,128]{2,1,0:T(8,128)(2,1)S(1)}, bf16[10,128,128]{2,1,0:T(8,128)(2,1)S(1)}, u32[]{:S(2)}, u32[]{:S(2)}) collective-permute-start(bf16[10,128,128]{2,1,0:T(8,128)(2,1)S(1)} %pad_maximum_fusion), channel_id=1, source_target_pairs={{0,8},{8,16},{16,24},{24,0},{1,9},{9,17},{17,25},{25,1},{2,10},{10... | collective-permute-start | bytes 983048 | tf_op jit(solution)/shard_map/ppermute | solution.py:61
  22.6 1.9 %collective-permute-start.9 = (bf16[10,128,128]{2,1,0:T(8,128)(2,1)S(1)}, bf16[10,128,128]{2,1,0:T(8,128)(2,1)S(1)}, u32[]{:S(2)}, u32[]{:S(2)}) collective-permute-start(bf16[10,128,128]{2,1,0:T(8,128)(2,1)S(1)} %pad_maximum_fusion.1), channel_id=1, source_target_pairs={{0,24},{8,0},{16,8},{24,16},{1,25},{9,1},{17,9},{25,17},{2,26},{10... | collective-permute-start | bytes 983048 | tf_op jit(solution)/shard_map/ppermute | solution.py:61
  24.5 2.8 %fine_ends.1 = (f32[2,2,4,16,256]{4,3,2,1,0:T(8,128)S(1)}, f32[2,2,4,16,256]{4,3,2,1,0:T(8,128)S(1)}, f32[2,2,6,16,256]{4,3,2,1,0:T(8,128)S(1)}) custom-call(bf16[8,128,128]{2,1,0:T(8,128)(2,1)S(1)} %collective-permute-done.6.zlo, bf16[8,8,128,128]{3,2,1,0:T(8,128)(2,1)S(1)} %get-tuple-element.17.block, bf16[8,128,128]{2,1,0:T(8,128)(2,1)S(1)} %collective-permute-done.7.zhi, ...), custom_call_target="tpu_custom_call" | custom-call | flops 2548039680 | bytes 5242880 | tf_op jit(solution)/shard_map/fine_ends/pallas_call | solution.py:149
  27.3 0.0 copy-start.5
  27.3 1.7 %fine_faces.1.facc = f32[2,8,8,16,256]{4,3,2,1,0:T(8,128)S(1)} custom-call(s32[1]{0:T(128)} %bitcast.odd, bf16[8,8,16,128]{3,2,1,0:T(8,128)(2,1)S(1)} %collective-permute-done.got_a, bf16[8,8,16,128]{3,2,1,0:T(8,128)(2,1)S(1)} %collective-permute-done.1.got_b, bf16[9,3,128,256]{3,2,1,0:T(8,128)(2,1)S(1)} %bitcast.37, ...), custom_call_target="tpu_custom_call" | custom-call | flops 1207959552 | bytes 6291456 | tf_op jit(solution)/shard_map/fine_faces/pallas_call | solution.py:269
  29.0 0.0 collective-permute-done.2.zlo
  29.1 0.0 collective-permute-done.3.zhi
  29.1 0.4 collective-permute-start.4
  29.6 2.9 %collective-permute-start.5 = (bf16[20,16,128]{2,1,0:T(8,128)(2,1)S(1)}, bf16[20,16,128]{2,1,0:T(8,128)(2,1)S(1)}, u32[]{:S(2)}, u32[]{:S(2)}) collective-permute-start(bf16[20,16,128]{2,1,0:T(8,128)(2,1)S(1)} %get-tuple-element.47), channel_id=1, source_target_pairs={{0,24},{8,0},{16,8},{24,16},{1,25},{9,1},{17,9},{25,17},{2,26},{10... | collective-permute-start | bytes 245768 | tf_op jit(solution)/shard_map/ppermute | solution.py:61
  32.4 0.0 collective-permute-done.8.xlo
  32.5 0.7 collective-permute-done.9.xhi
  33.1 0.0 copy-done.5
  33.1 5.2 %fine_sides.1 = (bf16[16,32,256]{2,1,0:T(8,128)(2,1)S(1)}, f32[2,4,4,16,256]{4,3,2,1,0:T(8,128)S(1)}, f32[2,8,2,16,256]{4,3,2,1,0:T(8,128)S(1)}) custom-call(bf16[10,128,128]{2,1,0:T(8,128)(2,1)S(1)} %collective-permute-done.8.xlo, bf16[10,128,128]{2,1,0:T(8,128)(2,1)S(1)} %collective-permute-done.9.xhi, ...), custom_call_target="tpu_custom_call" | custom-call | flops 3510632448 | bytes 5242880 | tf_op jit(solution)/shard_map/fine_sides/pallas_call | solution.py:149
  38.4 0.0 collective-permute-done.4.xlo
  38.4 0.0 collective-permute-done.5.xhi
  38.4 0.0 copy-start.1
  38.4 0.0 copy-start.3
  38.4 0.7 fine_last.1
  39.2 15.3 %all_to_all.10.got = bf16[16,64,256]{2,1,0:T(8,128)(2,1)S(1)} all-to-all(bf16[16,64,256]{2,1,0:T(8,128)(2,1)S(1)} %fine_last.1), channel_id=1, replica_groups=mesh['sample'=4,'space'=4,'chan'=8] {'sample','space'}, dimensions={0} | all-to-all | bytes 1048576 | tf_op jit(solution)/shard_map/all_to_all | solution.py:453
  54.5 2.3 %collective-permute-start.10 = (bf16[16,16,256]{2,1,0:T(8,128)(2,1)S(1)}, bf16[16,16,256]{2,1,0:T(8,128)(2,1)S(1)}, u32[]{:S(2)}, u32[]{:S(2)}) collective-permute-start(bf16[16,16,256]{2,1,0:T(8,128)(2,1)S(1)} %get-tuple-element.34), channel_id=1, source_target_pairs={{0,7},{1,2},{2,1},{3,4},{4,3},{5,6},{6,5},{7,0},{8,15},{9,10},{10,... | collective-permute-start | bytes 393224 | tf_op jit(solution)/shard_map/ppermute | solution.py:70
  56.8 0.0 collective-permute-start.11
  56.8 0.0 copy-done.1
  56.8 0.0 copy-done.3
  56.8 0.0 copy-start.4
  56.8 3.5 %deep_first.1.acc_in = f32[4,4,4,16,256]{4,3,2,1,0:T(8,128)S(1)} custom-call(bf16[16,64,256]{2,1,0:T(8,128)(2,1)S(1)} %all_to_all.10.got, bf16[576,256]{1,0:T(8,128)(2,1)S(1)} %copy-done.3, bf16[9,3,256,256]{3,2,1,0:T(8,128)(2,1)S(1)} %bitcast.40), custom_call_target="tpu_custom_call" | custom-call | flops 3623878656 | bytes 6291456 | tf_op jit(solution)/shard_map/deep_first/pallas_call | solution.py:341
  60.4 3.2 %collective-permute-done.10.got_a = bf16[16,16,256]{2,1,0:T(8,128)(2,1)S(1)} collective-permute-done((bf16[16,16,256]{2,1,0:T(8,128)(2,1)S(1)}, bf16[16,16,256]{2,1,0:T(8,128)(2,1)S(1)}, u32[]{:S(2)}, u32[]{:S(2)}) %collective-permute-start.10) | collective-permute-done | bytes 131104 | tf_op jit(solution)/shard_map/ppermute | solution.py:70
  63.6 0.0 collective-permute-done.11.got_b
  63.6 0.0 copy-done.4
  63.6 1.9 %deep_last.1 = bf16[8,256,128]{2,1,0:T(8,128)(2,1)S(1)} custom-call(s32[1]{0:T(128)} %bitcast.odd, bf16[16,16,256]{2,1,0:T(8,128)(2,1)S(1)} %collective-permute-done.10.got_a, bf16[16,16,256]{2,1,0:T(8,128)(2,1)S(1)} %collective-permute-done.11.got_b, bf16[576,256]{1,0:T(8,128)(2,1)S(1)} %copy-done.3, bf16[9,3,256,256]{3,2,1,0:T(8,128)(2,1)S(1)} %bitcast.41, ...), custom_call_target="tpu_custom_call" | custom-call | flops 603979776 | bytes 6291456 | tf_op jit(solution)/shard_map/deep_last/pallas_call | solution.py:379
  65.5 14.1 %all_to_all.11.got = bf16[8,256,128]{2,1,0:T(8,128)(2,1)S(1)} all-to-all(bf16[8,256,128]{2,1,0:T(8,128)(2,1)S(1)} %deep_last.1), channel_id=1, replica_groups=mesh['sample'=4,'space'=4,'chan'=8] {'chan'}, dimensions={0} | all-to-all | bytes 1048576 | tf_op jit(solution)/shard_map/all_to_all | solution.py:460
  79.6 0.0 copy-done.2
  79.6 1.3 %arrange.1 = bf16[1,32,16,512]{3,2,1,0:T(8,128)(2,1)} custom-call(bf16[8,256,128]{2,1,0:T(8,128)(2,1)S(1)} %all_to_all.11.got, bf16[512,512]{1,0:T(8,128)(2,1)S(1)} %copy-done.2), custom_call_target="tpu_custom_call" | custom-call | flops 268435456 | bytes 1048576 | tf_op jit(solution)/shard_map/arrange/pallas_call | solution.py:407
  (18 shorter events, 0.3 us)
Async XLA Ops:
  0.0 1.6 %copy-start.6 = (bf16[16,8,8,8,128]{4,3,2,1,0:T(8,128)(2,1)S(1)}, bf16[16,8,8,8,128]{4,3,2,1,0:T(8,128)(2,1)}, u32[]{:S(2)}) copy-start(bf16[16,8,8,8,128]{4,3,2,1,0:T(8,128)(2,1)} %param.7) | copy-start | bytes 6291460
  1.6 9.2 %copy-start = (bf16[3,3,3,128,256]{4,3,2,1,0:T(8,128)(2,1)S(1)}, bf16[3,3,3,128,256]{4,3,2,1,0:T(8,128)(2,1)}, u32[]{:S(2)}) copy-start(bf16[3,3,3,128,256]{4,3,2,1,0:T(8,128)(2,1)} %param.8) | copy-start | bytes 5308420
  2.4 16.5 %collective-permute-start = (bf16[8,8,16,128]{3,2,1,0:T(8,128)(2,1)S(1)}, bf16[8,8,16,128]{3,2,1,0:T(8,128)(2,1)S(1)}, u32[]{:S(2)}, u32[]{:S(2)}) collective-permute-start(bf16[8,8,16,128]{3,2,1,0:T(8,128)(2,1)S(1)} %get-tuple-element.31), channel_id=1, source_target_pairs={{0,7},{1,2},{2,1},{3,4},{4,3},{5,6},{6,5},{7,0},{8,15},{9,10},{10,... | collective-permute-start | bytes 786440 | tf_op jit(solution)/shard_map/ppermute | solution.py:70
  9.0 9.9 %collective-permute-start.1 = (bf16[8,8,16,128]{3,2,1,0:T(8,128)(2,1)S(1)}, bf16[8,8,16,128]{3,2,1,0:T(8,128)(2,1)S(1)}, u32[]{:S(2)}, u32[]{:S(2)}) collective-permute-start(bf16[8,8,16,128]{3,2,1,0:T(8,128)(2,1)S(1)} %get-tuple-element.32), channel_id=1, source_target_pairs={{0,1},{1,0},{2,3},{3,2},{4,5},{5,4},{6,7},{7,6},{8,9},{9,8},{10,11... | collective-permute-start | bytes 786440 | tf_op jit(solution)/shard_map/ppermute | solution.py:70
  9.0 11.8 %collective-permute-start.6 = (bf16[8,128,128]{2,1,0:T(8,128)(2,1)S(1)}, bf16[8,128,128]{2,1,0:T(8,128)(2,1)S(1)}, u32[]{:S(2)}, u32[]{:S(2)}) collective-permute-start(bf16[8,128,128]{2,1,0:T(8,128)(2,1)S(1)} %get-tuple-element.19), channel_id=1, source_target_pairs={{0,32},{32,64},{64,96},{96,0},{1,33},{33,65},{65,97},{97,1},{2,34}... | collective-permute-start | bytes 786440 | tf_op jit(solution)/shard_map/ppermute | solution.py:61
  9.0 11.8 %collective-permute-start.7 = (bf16[8,128,128]{2,1,0:T(8,128)(2,1)S(1)}, bf16[8,128,128]{2,1,0:T(8,128)(2,1)S(1)}, u32[]{:S(2)}, u32[]{:S(2)}) collective-permute-start(bf16[8,128,128]{2,1,0:T(8,128)(2,1)S(1)} %get-tuple-element.20), channel_id=1, source_target_pairs={{0,96},{32,0},{64,32},{96,64},{1,97},{33,1},{65,33},{97,65},{2,98}... | collective-permute-start | bytes 786440 | tf_op jit(solution)/shard_map/ppermute | solution.py:61
  18.9 10.1 %collective-permute-start.2 = (bf16[16,16,128]{2,1,0:T(8,128)(2,1)S(1)}, bf16[16,16,128]{2,1,0:T(8,128)(2,1)S(1)}, u32[]{:S(2)}, u32[]{:S(2)}) collective-permute-start(bf16[16,16,128]{2,1,0:T(8,128)(2,1)S(1)} %pad_maximum_fusion.2), channel_id=1, source_target_pairs={{0,32},{32,64},{64,96},{96,0},{1,33},{33,65},{65,97},{97,1},{2,34}... | collective-permute-start | bytes 196616 | tf_op jit(solution)/shard_map/ppermute | solution.py:61
  19.0 10.0 %collective-permute-start.3 = (bf16[16,16,128]{2,1,0:T(8,128)(2,1)S(1)}, bf16[16,16,128]{2,1,0:T(8,128)(2,1)S(1)}, u32[]{:S(2)}, u32[]{:S(2)}) collective-permute-start(bf16[16,16,128]{2,1,0:T(8,128)(2,1)S(1)} %pad_maximum_fusion.3), channel_id=1, source_target_pairs={{0,96},{32,0},{64,32},{96,64},{1,97},{33,1},{65,33},{97,65},{2,98}... | collective-permute-start | bytes 196616 | tf_op jit(solution)/shard_map/ppermute | solution.py:61
  20.9 11.5 %collective-permute-start.8 = (bf16[10,128,128]{2,1,0:T(8,128)(2,1)S(1)}, bf16[10,128,128]{2,1,0:T(8,128)(2,1)S(1)}, u32[]{:S(2)}, u32[]{:S(2)}) collective-permute-start(bf16[10,128,128]{2,1,0:T(8,128)(2,1)S(1)} %pad_maximum_fusion), channel_id=1, source_target_pairs={{0,8},{8,16},{16,24},{24,0},{1,9},{9,17},{17,25},{25,1},{2,10},{10... | collective-permute-start | bytes 983048 | tf_op jit(solution)/shard_map/ppermute | solution.py:61
  22.6 10.5 %collective-permute-start.9 = (bf16[10,128,128]{2,1,0:T(8,128)(2,1)S(1)}, bf16[10,128,128]{2,1,0:T(8,128)(2,1)S(1)}, u32[]{:S(2)}, u32[]{:S(2)}) collective-permute-start(bf16[10,128,128]{2,1,0:T(8,128)(2,1)S(1)} %pad_maximum_fusion.1), channel_id=1, source_target_pairs={{0,24},{8,0},{16,8},{24,16},{1,25},{9,1},{17,9},{25,17},{2,26},{10... | collective-permute-start | bytes 983048 | tf_op jit(solution)/shard_map/ppermute | solution.py:61
  27.3 5.8 %copy-start.5 = (f32[256]{0:T(256)S(1)}, f32[256]{0:T(256)}, u32[]{:S(2)}) copy-start(f32[256]{0:T(256)} %param.9) | copy-start | bytes 3076
  29.1 9.2 %collective-permute-start.4 = (bf16[20,16,128]{2,1,0:T(8,128)(2,1)S(1)}, bf16[20,16,128]{2,1,0:T(8,128)(2,1)S(1)}, u32[]{:S(2)}, u32[]{:S(2)}) collective-permute-start(bf16[20,16,128]{2,1,0:T(8,128)(2,1)S(1)} %get-tuple-element.48), channel_id=1, source_target_pairs={{0,8},{8,16},{16,24},{24,0},{1,9},{9,17},{17,25},{25,1},{2,10},{10... | collective-permute-start | bytes 245768 | tf_op jit(solution)/shard_map/ppermute | solution.py:61
  29.6 8.8 %collective-permute-start.5 = (bf16[20,16,128]{2,1,0:T(8,128)(2,1)S(1)}, bf16[20,16,128]{2,1,0:T(8,128)(2,1)S(1)}, u32[]{:S(2)}, u32[]{:S(2)}) collective-permute-start(bf16[20,16,128]{2,1,0:T(8,128)(2,1)S(1)} %get-tuple-element.47), channel_id=1, source_target_pairs={{0,24},{8,0},{16,8},{24,16},{1,25},{9,1},{17,9},{25,17},{2,26},{10... | collective-permute-start | bytes 245768 | tf_op jit(solution)/shard_map/ppermute | solution.py:61
  38.4 18.4 %copy-start.1 = (bf16[3,3,3,256,256]{4,3,2,1,0:T(8,128)(2,1)S(1)}, bf16[3,3,3,256,256]{4,3,2,1,0:T(8,128)(2,1)}, u32[]{:S(2)}) copy-start(bf16[3,3,3,256,256]{4,3,2,1,0:T(8,128)(2,1)} %param.10) | copy-start | bytes 10616836
  38.4 18.4 %copy-start.3 = (bf16[576,256]{1,0:T(8,128)(2,1)S(1)}, bf16[576,256]{1,0:T(8,128)(2,1)}, u32[]{:S(2)}) copy-start(bf16[576,256]{1,0:T(8,128)(2,1)} %constant.22.clone.pad) | copy-start | bytes 884740
  54.5 9.0 %collective-permute-start.10 = (bf16[16,16,256]{2,1,0:T(8,128)(2,1)S(1)}, bf16[16,16,256]{2,1,0:T(8,128)(2,1)S(1)}, u32[]{:S(2)}, u32[]{:S(2)}) collective-permute-start(bf16[16,16,256]{2,1,0:T(8,128)(2,1)S(1)} %get-tuple-element.34), channel_id=1, source_target_pairs={{0,7},{1,2},{2,1},{3,4},{4,3},{5,6},{6,5},{7,0},{8,15},{9,10},{10,... | collective-permute-start | bytes 393224 | tf_op jit(solution)/shard_map/ppermute | solution.py:70
  56.8 6.7 %collective-permute-start.11 = (bf16[16,16,256]{2,1,0:T(8,128)(2,1)S(1)}, bf16[16,16,256]{2,1,0:T(8,128)(2,1)S(1)}, u32[]{:S(2)}, u32[]{:S(2)}) collective-permute-start(bf16[16,16,256]{2,1,0:T(8,128)(2,1)S(1)} %get-tuple-element.33), channel_id=1, source_target_pairs={{0,1},{1,0},{2,3},{3,2},{4,5},{5,4},{6,7},{7,6},{8,9},{9,8},{10,11... | collective-permute-start | bytes 393224 | tf_op jit(solution)/shard_map/ppermute | solution.py:70
  56.8 6.7 %copy-start.4 = (f32[256]{0:T(256)S(1)}, f32[256]{0:T(256)}, u32[]{:S(2)}) copy-start(f32[256]{0:T(256)} %param.11) | copy-start | bytes 3076
  63.6 16.0 %copy-start.2 = (bf16[512,512]{1,0:T(8,128)(2,1)S(1)}, bf16[512,512]{1,0:T(8,128)(2,1)}, u32[]{:S(2)}) copy-start(bf16[512,512]{1,0:T(8,128)(2,1)} %constant.23.clone.lanes) | copy-start | bytes 1572868
